TPU v7x, 32 devices: a whole 2x2x4 slice. The times are simulated.
32 devices in a mesh: sta: 4 (over z), tm: 8 (over y, x, core).
Axes of the slice: x: 2, y: 2, z: 4, core: 2. Of those that a mesh axis runs over, the one named last changes fastest.
Arguments:
- waveforms: bfloat16 [16, 3, 16384], P('sta', None, 'tm'), may hold values from -90 to 90, as said below
- templates: bfloat16 [16, 768, 256], P('sta'), may hold values from -21 to 21
- moveouts: int32 [16, 256], P('sta'), may hold values from 0 to 1791, as said below
- gap_masks: int32 [16, 8], P('sta'), may hold values 0 or 1
Outputs:
- stack: float32 [256, 16384], P('sta', 'tm')
Inputs may be any that keep to these rules, and one draw needn't show every extreme that they name: `waveforms`: each waveform sample lies within -90 to 90. `moveouts`: moveouts are whole sample counts, below 1792.
All inputs are finite; a program needn't handle non-finite values. No bound on the sum of `gap_masks` on one device may be relied on, other than what follows from the above.
Results may differ from a plain program's by a relative error of at most 0.0003.
Values may be sent and summed in bfloat16 or wider, within the bound.
A program may use at most 64 MiB of HBM per device.

v0:
```python
import jax
import jax.numpy as jnp
from jax import lax
from jax.sharding import PartitionSpec as P

TLEN = 256
NTEMP = 256
MAXMOVE = 1792
BLOCK = 2048


EPSILON = 1e-06


def shifted(block, axis, distance):
    devices = range(lax.axis_size(axis))
    route = [(i - distance, i) for i in devices if i - distance in devices]
    return lax.ppermute(block, axis, route)


def hankel(series, row_count):
    length = series.shape[-1]
    repeated = jnp.tile(series, (1,) * (series.ndim - 1) + (TLEN + 1,))
    flattened = repeated[..., : TLEN * (length + 1)]
    return flattened.reshape(series.shape[:-1] + (TLEN, length + 1))[..., :row_count]


def correlate(signal, template_s, row_count):
    hankel_mat = hankel(signal, row_count).reshape(3 * TLEN, row_count)
    product = lax.dot_general(
        template_s, hankel_mat, (((0,), (0,)), ((), ())), preferred_element_type=jnp.float32
    )
    squares = jnp.sum(signal.astype(jnp.float32) ** 2, axis=0)
    energy = jnp.sum(hankel(squares, row_count), axis=0) / (3 * TLEN)
    tmpl_energy = jnp.mean(template_s.astype(jnp.float32) ** 2, axis=0)
    scaling = 3 * TLEN * jnp.sqrt((energy + EPSILON)[None, :] * (tmpl_energy + EPSILON)[:, None])
    return product / scaling


def shift_rows(padded, lag_row, out_rows):
    bit_count = max(1, (MAXMOVE - 1).bit_length())
    current = jnp.concatenate(
        [padded, jnp.zeros((padded.shape[0], 1 << bit_count), jnp.float32)], axis=1
    )
    for bit_pos in range(bit_count):
        stride = 1 << bit_pos
        taken = lag_row >> bit_pos & 1 == 1
        current = jnp.where(taken[:, None], current[:, stride:], current[:, :-stride])
    return current[:, :out_rows]


def local(waveforms, templates, moveouts, gap_masks):
    sta_count = waveforms.shape[0]
    send_len = MAXMOVE + TLEN
    row_count = BLOCK + MAXMOVE
    front_pad = 0
    out_rows = BLOCK
    following = shifted(waveforms, "tm", -1)
    extended = jnp.concatenate([waveforms, following[:, :, : row_count - BLOCK + TLEN - 1]], axis=2)
    position = lax.axis_index("tm")
    blk_count = gap_masks.shape[1]
    current = lax.dynamic_slice_in_dim(gap_masks, position, 1, axis=1).astype(jnp.float32)
    later = lax.dynamic_slice_in_dim(
        gap_masks, jnp.minimum(position + 1, blk_count - 1), 1, axis=1
    ).astype(jnp.float32)
    alive_rows = jnp.concatenate(
        [
            jnp.broadcast_to(current, (sta_count, BLOCK)),
            jnp.broadcast_to(later, (sta_count, row_count - BLOCK)),
        ],
        axis=1,
    )

    def station(station_idx, running):
        signal = lax.dynamic_index_in_dim(extended, station_idx, 0, keepdims=False)
        template_s = lax.dynamic_index_in_dim(templates, station_idx, 0, keepdims=False)
        lag_row = lax.dynamic_index_in_dim(moveouts, station_idx, 0, keepdims=False)
        alive_row = lax.dynamic_index_in_dim(alive_rows, station_idx, 0, keepdims=False)
        normalized = correlate(signal, template_s, row_count) * alive_row[None, :]
        padding = jnp.zeros((NTEMP, front_pad), jnp.float32)
        padded = jnp.concatenate([padding, normalized, padding], axis=1)
        return running + shift_rows(padded, lag_row, out_rows)

    stacked = lax.fori_loop(0, sta_count, station, jnp.zeros((NTEMP, out_rows), jnp.float32))
    reduced = lax.psum_scatter(stacked, "sta", scatter_dimension=0, tiled=True)
    return reduced


def solution(mesh):
    in_specs = (P("sta", None, "tm"), P("sta", None, None), P("sta", None), P("sta", None))
    out_specs = P("sta", "tm")
    return jax.shard_map(local, mesh=mesh, in_specs=in_specs, out_specs=out_specs, check_vma=False)
```

profile of v0, /device:TPU:0, one launch (start us, length us, event | category | flops | bytes accessed | tf_op | source)
XLA Modules:
  0.0 455.2 jit_solution(6015050647290760645)
XLA Ops:
  10.6 387.4 %while.14 = (s32[]{:T(128)}, f32[256,2048]{1,0:T(8,128)S(1)}, s32[4,256]{1,0:T(4,128)}, bf16[4,768,256]{2,1,0:T(8,128)(2,1)}, bf16[4,3,4095]{2,1,0:T(4,128)(2,1)...) while((s32[]{:T(128)}, f32[256,2048]{1,0:T(8,128)S(1)}, s32[4,256]{1,0:T(4,128)}, ...), condition=%wide.region_4.5_spmd.clone, body=%wide.region_0.4_spmd.clone.sunk | while | flops 1531624704 | bytes 313822752 | solution.py:84
  34.4 3.5 tile.55
  37.9 11.9 %reshape.227 = bf16[3157245]{0:T(1024)(128)(2,1)} reshape(bf16[3,257,4095]{2,1,0:T(8,128)(2,1)} %tile.55) | data formatting | bytes 12628980 | tf_op jit(solution)/shard_map/while
  49.8 10.0 %tile.56 = bf16[3,1052415]{1,0:T(4,128)(2,1)} reshape(bf16[3157245]{0:T(1024)(128)(2,1)} %reshape.227) | data formatting | bytes 12628980 | tf_op jit(solution)/shard_map/while/body/eval_jaxpr/tile | solution.py:23
  59.8 3.4 slice-done
  63.2 7.2 %copy.13 = bf16[1,3,256,4096]{3,2,1,0:T(8,128)(2,1)} copy(bf16[1,3,256,4096]{3,1,2,0:T(4,128)(2,1)S(1)} %bitcast.26) | data formatting | bytes 12582912 | tf_op jit(solution)/shard_map/while
  70.4 5.6 %slice.332 = bf16[3,256,3840]{2,1,0:T(8,128)(2,1)} slice(bf16[3,256,4096]{2,1,0:T(8,128)(2,1)} %bitcast.27), slice={[0:3], [0:256], [0:3840]} | slice | bytes 11796480 | tf_op jit(solution)/shard_map/while/body/eval_jaxpr/slice | solution.py:25
  78.6 5.9 %tile.58 = f32[1052415]{0:T(1024)} reshape(f32[257,4095]{1,0:T(8,128)} %tile.57) | data formatting | bytes 8419320 | tf_op jit(solution)/shard_map/while/body/eval_jaxpr/tile | solution.py:23
  84.5 4.5 slice.333
  89.0 5.0 %reshape.228 = f32[256,4096]{1,0:T(8,128)} reshape(f32[1048576]{0:T(1024)} %slice.333) | data formatting | bytes 8388608 | tf_op jit(solution)/shard_map/while/body/eval_jaxpr/reshape | solution.py:25
  97.5 5.7 %fusion.16 = f32[256,3840]{1,0:T(8,128)S(1)} fusion(bf16[768,3840]{1,0:T(8,128)(2,1)} %bitcast.28, f32[3840]{0:T(1024)S(1)} %dynamic-slice_reduce_fusion.2, f32[256]{0:T(256)S(1)} %multiply_add_fusion.4, f32[3840]{0:T(1024)S(1)} %multiply_add_fusion.5, bf16[4,768,256]{2,1,0:T(8,128)(2,1)} %get-tuple-element.251, s32[]{:T(128)} %get-tuple-element.240), kind=kOutput, calls=%fused_computation.14.clone.1 | convolution fusion | flops 1513881600 | bytes 10255872 | tf_op jit(solution)/shard_map/while/body/eval_jaxpr/dot_general | solution.py:30
  118.8 3.7 fusion.18
  125.3 3.5 tile.55
  128.8 11.9 %reshape.227 = bf16[3157245]{0:T(1024)(128)(2,1)} reshape(bf16[3,257,4095]{2,1,0:T(8,128)(2,1)} %tile.55) | data formatting | bytes 12628980 | tf_op jit(solution)/shard_map/while
  140.7 10.0 %tile.56 = bf16[3,1052415]{1,0:T(4,128)(2,1)} reshape(bf16[3157245]{0:T(1024)(128)(2,1)} %reshape.227) | data formatting | bytes 12628980 | tf_op jit(solution)/shard_map/while/body/eval_jaxpr/tile | solution.py:23
  150.7 3.4 slice-done
  154.1 7.2 %copy.13 = bf16[1,3,256,4096]{3,2,1,0:T(8,128)(2,1)} copy(bf16[1,3,256,4096]{3,1,2,0:T(4,128)(2,1)S(1)} %bitcast.26) | data formatting | bytes 12582912 | tf_op jit(solution)/shard_map/while
  161.3 5.6 %slice.332 = bf16[3,256,3840]{2,1,0:T(8,128)(2,1)} slice(bf16[3,256,4096]{2,1,0:T(8,128)(2,1)} %bitcast.27), slice={[0:3], [0:256], [0:3840]} | slice | bytes 11796480 | tf_op jit(solution)/shard_map/while/body/eval_jaxpr/slice | solution.py:25
  169.5 5.9 %tile.58 = f32[1052415]{0:T(1024)} reshape(f32[257,4095]{1,0:T(8,128)} %tile.57) | data formatting | bytes 8419320 | tf_op jit(solution)/shard_map/while/body/eval_jaxpr/tile | solution.py:23
  175.4 4.5 slice.333
  179.9 5.0 %reshape.228 = f32[256,4096]{1,0:T(8,128)} reshape(f32[1048576]{0:T(1024)} %slice.333) | data formatting | bytes 8388608 | tf_op jit(solution)/shard_map/while/body/eval_jaxpr/reshape | solution.py:25
  188.5 5.7 %fusion.16 = f32[256,3840]{1,0:T(8,128)S(1)} fusion(bf16[768,3840]{1,0:T(8,128)(2,1)} %bitcast.28, f32[3840]{0:T(1024)S(1)} %dynamic-slice_reduce_fusion.2, f32[256]{0:T(256)S(1)} %multiply_add_fusion.4, f32[3840]{0:T(1024)S(1)} %multiply_add_fusion.5, bf16[4,768,256]{2,1,0:T(8,128)(2,1)} %get-tuple-element.251, s32[]{:T(128)} %get-tuple-element.240), kind=kOutput, calls=%fused_computation.14.clone.1 | convolution fusion | flops 1513881600 | bytes 10255872 | tf_op jit(solution)/shard_map/while/body/eval_jaxpr/dot_general | solution.py:30
  209.7 3.7 fusion.18
  213.3 2.8 fusion.19
  216.2 3.5 tile.55
  219.7 11.9 %reshape.227 = bf16[3157245]{0:T(1024)(128)(2,1)} reshape(bf16[3,257,4095]{2,1,0:T(8,128)(2,1)} %tile.55) | data formatting | bytes 12628980 | tf_op jit(solution)/shard_map/while
  231.7 10.0 %tile.56 = bf16[3,1052415]{1,0:T(4,128)(2,1)} reshape(bf16[3157245]{0:T(1024)(128)(2,1)} %reshape.227) | data formatting | bytes 12628980 | tf_op jit(solution)/shard_map/while/body/eval_jaxpr/tile | solution.py:23
  241.7 3.4 slice-done
  245.1 7.2 %copy.13 = bf16[1,3,256,4096]{3,2,1,0:T(8,128)(2,1)} copy(bf16[1,3,256,4096]{3,1,2,0:T(4,128)(2,1)S(1)} %bitcast.26) | data formatting | bytes 12582912 | tf_op jit(solution)/shard_map/while
  252.2 5.6 %slice.332 = bf16[3,256,3840]{2,1,0:T(8,128)(2,1)} slice(bf16[3,256,4096]{2,1,0:T(8,128)(2,1)} %bitcast.27), slice={[0:3], [0:256], [0:3840]} | slice | bytes 11796480 | tf_op jit(solution)/shard_map/while/body/eval_jaxpr/slice | solution.py:25
  260.4 5.9 %tile.58 = f32[1052415]{0:T(1024)} reshape(f32[257,4095]{1,0:T(8,128)} %tile.57) | data formatting | bytes 8419320 | tf_op jit(solution)/shard_map/while/body/eval_jaxpr/tile | solution.py:23
  266.3 4.5 slice.333
  270.8 5.0 %reshape.228 = f32[256,4096]{1,0:T(8,128)} reshape(f32[1048576]{0:T(1024)} %slice.333) | data formatting | bytes 8388608 | tf_op jit(solution)/shard_map/while/body/eval_jaxpr/reshape | solution.py:25
  279.4 5.7 %fusion.16 = f32[256,3840]{1,0:T(8,128)S(1)} fusion(bf16[768,3840]{1,0:T(8,128)(2,1)} %bitcast.28, f32[3840]{0:T(1024)S(1)} %dynamic-slice_reduce_fusion.2, f32[256]{0:T(256)S(1)} %multiply_add_fusion.4, f32[3840]{0:T(1024)S(1)} %multiply_add_fusion.5, bf16[4,768,256]{2,1,0:T(8,128)(2,1)} %get-tuple-element.251, s32[]{:T(128)} %get-tuple-element.240), kind=kOutput, calls=%fused_computation.14.clone.1 | convolution fusion | flops 1513881600 | bytes 10255872 | tf_op jit(solution)/shard_map/while/body/eval_jaxpr/dot_general | solution.py:30
  300.6 3.7 fusion.18
  304.3 2.8 fusion.19
  307.1 3.5 tile.55
  310.6 11.9 %reshape.227 = bf16[3157245]{0:T(1024)(128)(2,1)} reshape(bf16[3,257,4095]{2,1,0:T(8,128)(2,1)} %tile.55) | data formatting | bytes 12628980 | tf_op jit(solution)/shard_map/while
  322.6 10.0 %tile.56 = bf16[3,1052415]{1,0:T(4,128)(2,1)} reshape(bf16[3157245]{0:T(1024)(128)(2,1)} %reshape.227) | data formatting | bytes 12628980 | tf_op jit(solution)/shard_map/while/body/eval_jaxpr/tile | solution.py:23
  332.6 3.4 slice-done
  336.0 7.2 %copy.13 = bf16[1,3,256,4096]{3,2,1,0:T(8,128)(2,1)} copy(bf16[1,3,256,4096]{3,1,2,0:T(4,128)(2,1)S(1)} %bitcast.26) | data formatting | bytes 12582912 | tf_op jit(solution)/shard_map/while
  343.2 5.6 %slice.332 = bf16[3,256,3840]{2,1,0:T(8,128)(2,1)} slice(bf16[3,256,4096]{2,1,0:T(8,128)(2,1)} %bitcast.27), slice={[0:3], [0:256], [0:3840]} | slice | bytes 11796480 | tf_op jit(solution)/shard_map/while/body/eval_jaxpr/slice | solution.py:25
  351.3 5.9 %tile.58 = f32[1052415]{0:T(1024)} reshape(f32[257,4095]{1,0:T(8,128)} %tile.57) | data formatting | bytes 8419320 | tf_op jit(solution)/shard_map/while/body/eval_jaxpr/tile | solution.py:23
  357.2 4.5 slice.333
  361.8 5.0 %reshape.228 = f32[256,4096]{1,0:T(8,128)} reshape(f32[1048576]{0:T(1024)} %slice.333) | data formatting | bytes 8388608 | tf_op jit(solution)/shard_map/while/body/eval_jaxpr/reshape | solution.py:25
  370.3 5.7 %fusion.16 = f32[256,3840]{1,0:T(8,128)S(1)} fusion(bf16[768,3840]{1,0:T(8,128)(2,1)} %bitcast.28, f32[3840]{0:T(1024)S(1)} %dynamic-slice_reduce_fusion.2, f32[256]{0:T(256)S(1)} %multiply_add_fusion.4, f32[3840]{0:T(1024)S(1)} %multiply_add_fusion.5, bf16[4,768,256]{2,1,0:T(8,128)(2,1)} %get-tuple-element.251, s32[]{:T(128)} %get-tuple-element.240), kind=kOutput, calls=%fused_computation.14.clone.1 | convolution fusion | flops 1513881600 | bytes 10255872 | tf_op jit(solution)/shard_map/while/body/eval_jaxpr/dot_general | solution.py:30
  391.5 3.7 fusion.18
  399.4 48.6 %reduce-scatter.2.cloned.1.call-done = f32[64,2048]{1,0:T(8,128)} async-done(((f32[256,2048]{1,0:T(8,128)}), f32[64,2048]{1,0:T(8,128)}) %reduce-scatter.2.cloned.1.call-update) | async-done | bytes 524304 | tf_op jit(solution)/shard_map/reduce_scatter | solution.py:85
  (91 shorter events, 97.4 us)
Async XLA Ops:
  6.5 441.4 %reduce-scatter.2.cloned.1.call-start = ((), (), s32[]{:S(2)}) async-start(), calls=%async_computation.1 | async-start | bytes 2621440 | tf_op jit(solution)/shard_map/reduce_scatter | solution.py:85
  7.4 3.1 collective-permute-start
  59.8 3.4 slice-start
  150.7 3.4 slice-start
  241.7 3.4 slice-start
  332.6 3.4 slice-start
  398.0 1.4 copy-start
Sparse Core Ops, SparseCore 0:
  399.5 48.4 reduce-scatter.1
where the time goes:
time: 458 us; the launch traced here: 455 us
  local copies, waits for them, and re-layouts  256 us (56%)
  other arithmetic  88 us (19%)
  waiting for transfers between devices  49.3 us (11%)
  loops' own time  24.2 us (5%)
  matrix products  22.9 us (5%)
  between operations  13.8 us (3%)
    another operation x16, local copies, waits for them, and re-layouts, hankel(): repeated = jnp.tile(series, (1,) * (series.ndim - 1) + (TLEN + 1,))  88.1 us
    while x8, local copies, waits for them, and re-layouts  76.5 us
    select_n x40, other arithmetic, shift_rows(): jnp.where(taken[:, None], current[:, stride:], current[:, :-stride])  58.7 us
    reduce_scatter x1, waiting for transfers between devices, local(): reduced = lax.psum_scatter(stacked, 'sta', scatter_dimension=0, tiled=True)  48.6 us
    slice x12, local copies, waits for them, and re-layouts, hankel(): flattened = repeated[..., :TLEN * (length + 1)]  31.6 us
    another operation x1, loops' own time, local(): lax.fori_loop(0, sta_count, station, jnp.zeros((NTEMP, out_rows), jnp.flo...  24.2 us
    dot_general x4, matrix products, correlate(): lax.dot_general(template_s, hankel_mat, (((0,), (0,)), ((), ())), preferr...  22.9 us
    slice x4, local copies, waits for them, and re-layouts, hankel(): flattened.reshape(series.shape[:-1] + (TLEN, length + 1))[..., :row_count]  22.3 us
  transfers between devices with their start and end apart: 2, of which 2 were waited for; matrix products, arithmetic and copies ran while one was open for 0% of the time, Pallas kernels for 0%

commit v1 on v0

v1 whole, which is shorter than its diff:
```python
import functools

import jax
import jax.numpy as jnp
from jax import lax
from jax.experimental import pallas as pl
from jax.experimental.pallas import tpu as pltpu
from jax.sharding import PartitionSpec as P

TLEN = 256
MAXMOVE = 1792
BLOCK = 2048
EPSILON = 1e-06
WIN = 2 * BLOCK
COLS = BLOCK + MAXMOVE
LANES = 128
ROWS = COLS // LANES
OUTR = BLOCK // LANES
TILE = 256


def shifted(block, axis, distance):
    devices = range(lax.axis_size(axis))
    route = [(i - distance, i) for i in devices if i - distance in devices]
    return lax.ppermute(block, axis, route)


def left(value, amount):
    size = value.shape[-1]
    return value if amount % size == 0 else pltpu.roll(value, (-amount) % size, axis=1)


def correlate_kernel(sta_count, ntemp, x_ref, w_ref, lag_ref, gap_ref, out_ref, hank, scale, corr, stack):
    groups = ntemp // 8
    corr_rows = groups * ROWS * 8

    def station(s, carry):
        wave = x_ref[s].astype(jnp.float32)
        run = jnp.sum(wave * wave, axis=0, keepdims=True)
        step = 1
        while step < TLEN:
            run = run + left(run, step)
            step *= 2
        row = lax.rsqrt(run / (3 * TLEN) + EPSILON) * (1.0 / (3 * TLEN))
        lane = lax.broadcasted_iota(jnp.int32, (1, WIN), 1)
        alive = jnp.where(lane < BLOCK, gap_ref[s, 0], gap_ref[s, 1]).astype(jnp.float32)
        scale[...] = jnp.broadcast_to(row * alive, (8, WIN))
        sub = lax.broadcasted_iota(jnp.int32, (16, WIN), 0)
        for c in range(3):
            base = jnp.broadcast_to(wave[c : c + 1], (16, WIN))
            for bit in (1, 2, 4, 8):
                base = jnp.where((sub & bit) != 0, left(base, bit), base)
            for a in range(8):
                hank[c, 16 * a : 16 * (a + 1), :] = left(base, 16 * a).astype(jnp.bfloat16)
        wt = w_ref[s]
        wf = wt.astype(jnp.float32)
        te = jnp.sum(wf * wf, axis=1, keepdims=True) / (3 * TLEN)
        tscale = lax.rsqrt(te + EPSILON)

        def tile(i, carry):
            start = pl.multiple_of(i * TILE, TILE)
            parts = []
            for c in range(3):
                parts.append(hank[c, :, pl.ds(start, TILE)])
                parts.append(hank[c, :, pl.ds(start + LANES, TILE)])
            rhs = jnp.concatenate(parts, axis=0)
            prod = lax.dot_general(wt, rhs, (((1,), (0,)), ((), ())), preferred_element_type=jnp.float32)
            prod = prod * tscale * scale[0:1, pl.ds(start, TILE)]
            for h in range(TILE // LANES):
                for g in range(groups):
                    at = s * corr_rows + g * ROWS * 8 + (i * (TILE // LANES) + h) * 8
                    corr[pl.ds(pl.multiple_of(at, 8), 8), :] = prod[8 * g : 8 * g + 8, LANES * h : LANES * (h + 1)]
            return carry

        lax.fori_loop(0, COLS // TILE, tile, 0)
        return carry

    lax.fori_loop(0, sta_count, station, 0)
    lanes = lax.broadcasted_iota(jnp.int32, (OUTR, LANES), 1)

    def group(g, carry):
        for k in range(8):
            total = None
            for s in range(sta_count):
                lag = lag_ref[s, g * 8 + k]
                p0 = lag // LANES
                r = lag % LANES
                at = s * corr_rows + (g * ROWS + p0) * 8 + k
                lo = corr[pl.ds(at, OUTR, stride=8), :]
                hi = corr[pl.ds(at + 8, OUTR, stride=8), :]
                term = pltpu.roll(jnp.where(lanes >= r, lo, hi), (LANES - r) % LANES, axis=1)
                total = term if total is None else total + term
            stack[pl.ds(k, OUTR, stride=8), :] = total
        for p in range(OUTR):
            out_ref[pl.ds(pl.multiple_of(g * 8, 8), 8), LANES * p : LANES * (p + 1)] = stack[8 * p : 8 * p + 8, :]
        return carry

    lax.fori_loop(0, groups, group, 0)


def correlated(extended, wt, lags, gaps):
    sta_count, ntemp = wt.shape[0], wt.shape[1]
    vmem = pl.BlockSpec(memory_space=pltpu.VMEM)
    smem = pl.BlockSpec(memory_space=pltpu.SMEM)
    return pl.pallas_call(
        functools.partial(correlate_kernel, sta_count, ntemp),
        out_shape=jax.ShapeDtypeStruct((ntemp, BLOCK), jnp.float32),
        in_specs=[vmem, vmem, smem, smem],
        out_specs=vmem,
        scratch_shapes=[
            pltpu.VMEM((3, LANES, WIN), jnp.bfloat16),
            pltpu.VMEM((8, WIN), jnp.float32),
            pltpu.VMEM((sta_count * ntemp * ROWS, LANES), jnp.float32),
            pltpu.VMEM((OUTR * 8, LANES), jnp.float32),
        ],
        compiler_params=pltpu.CompilerParams(vmem_limit_bytes=48 * 1024 * 1024),
        name="correlate",
    )(extended, wt, lags, gaps)


def local(waveforms, templates, moveouts, gap_masks):
    following = shifted(waveforms, "tm", -1)
    extended = jnp.concatenate([waveforms, following], axis=2)
    position = lax.axis_index("tm")
    last = gap_masks.shape[1] - 1
    current = lax.dynamic_slice_in_dim(gap_masks, position, 1, axis=1)
    later = lax.dynamic_slice_in_dim(gap_masks, jnp.minimum(position + 1, last), 1, axis=1)
    gaps = jnp.concatenate([current, later], axis=1)
    wt = jnp.transpose(templates, (0, 2, 1))
    stacked = correlated(extended, wt, moveouts, gaps)
    return lax.psum_scatter(stacked, "sta", scatter_dimension=0, tiled=True)


def solution(mesh):
    in_specs = (P("sta", None, "tm"), P("sta", None, None), P("sta", None), P("sta", None))
    out_specs = P("sta", "tm")
    return jax.shard_map(local, mesh=mesh, in_specs=in_specs, out_specs=out_specs, check_vma=False)
```

time: 458 us -> 105 us (0.23)
  local copies, waits for them, and re-layouts: 256 us -> 3.4 us
  other arithmetic: 88 us -> 0.14 us
  Pallas kernels: 0 us -> 38.8 us
  loops' own time: 24.2 us -> 0 us
  matrix products: 22.9 us -> 0 us
    another operation x16 -> x0, local copies, waits for them, and re-layouts: 88.1 us -> none  [hankel(): repeated = jnp.tile(series, (1,) * (series.ndim - 1) + (TLEN + 1,))]
    while x8 -> x0, local copies, waits for them, and re-layouts: 76.5 us -> none
    slice x20 -> x0, local copies, waits for them, and re-layouts: 68.5 us -> none  [the longest x12 31.6 us: hankel(): flattened = repeated[..., :TLEN * (length + 1)]]
    select_n x40 -> x0, other arithmetic: 58.7 us -> none  [shift_rows(): jnp.where(taken[:, None], current[:, stride:], current[:, :-stride])]
    pallas_call x0 -> x1, Pallas kernels: none -> 38.8 us  [correlated(): pl.pallas_call(functools.partial(correlate_kernel, sta_count, ntemp), out...]
    another operation x1 -> x0, loops' own time: 24.2 us -> none  [local(): lax.fori_loop(0, sta_count, station, jnp.zeros((NTEMP, out_rows), jnp.flo...]
    dot_general x4 -> x0, matrix products: 22.9 us -> none  [correlate(): lax.dot_general(template_s, hankel_mat, (((0,), (0,)), ((), ())), preferr...]
    reshape x4 -> x0, local copies, waits for them, and re-layouts: 20.1 us -> none  [hankel(): flattened.reshape(series.shape[:-1] + (TLEN, length + 1))[..., :row_count]]
  transfers between devices with their start and end apart: 2 -> 2, of which waited for: 2 -> 1; matrix products, arithmetic and copies ran while one was open for 0% -> 3% of each run, Pallas kernels for 0% -> 0%
where the time goes in v1:
time: 105 us
  waiting for transfers between devices  47.8 us (46%)
  Pallas kernels  38.8 us (37%)
  between operations  13.4 us (13%)
  local copies, waits for them, and re-layouts  3.4 us (3%)
  starting transfers between devices  1.29 us (1%)
    reduce_scatter x1, waiting for transfers between devices, local(): return lax.psum_scatter(stacked, 'sta', scatter_dimension=0, tiled=True)  47.8 us
    pallas_call x1, Pallas kernels, correlated(): pl.pallas_call(functools.partial(correlate_kernel, sta_count, ntemp), out...  38.8 us
    unnamed x4, local copies, waits for them, and re-layouts  2.57 us
  transfers between devices with their start and end apart: 2, of which 1 were waited for; matrix products, arithmetic and copies ran while one was open for 3% of the time, Pallas kernels for 0%

profile of v1, /device:TPU:0, one launch (start us, length us, event | category | flops | bytes accessed | tf_op | source)
XLA Modules:
  0.0 104.8 jit_solution(718479604067044547)
XLA Ops:
  6.5 0.0 reduce-scatter.2.cloned.1.call-start
  6.5 0.8 copy.6
  7.4 1.3 %collective-permute-start = (bf16[4,3,2048]{2,1,0:T(4,128)(2,1)S(1)}, bf16[4,3,2048]{2,1,0:T(4,128)(2,1)S(1)}, u32[]{:S(2)}, u32[]{:S(2)}) collective-permute-start(bf16[4,3,2048]{2,1,0:T(4,128)(2,1)S(1)} %copy.6), channel_id=1, source_target_pairs={{1,0},{2,1},{3,2},{4,3},{5,4},{6,5},{7,6},{9,8},{10,9},{11,10},{12... | collective-permute-start | bytes 147464 | tf_op jit(solution)/shard_map/ppermute | solution.py:25
  8.7 0.8 constant_dynamic-slice_fusion.1
  9.5 0.1 pad_add_fusion.gap_ref
  9.6 0.0 copy-start
  9.6 1.7 %copy.7 = bf16[4,768,256]{1,2,0:T(8,128)(2,1)S(1)} copy(bf16[4,768,256]{2,1,0:T(8,128)(2,1)} %param.5) | data formatting | bytes 3145728 | tf_op args[1]
  11.3 0.0 collective-permute-done
  11.3 0.1 pad_maximum_fusion.x_ref
  11.4 0.0 copy-done
  11.4 38.8 %correlate.1 = f32[256,2048]{1,0:T(8,128)} custom-call(bf16[4,3,4096]{2,1,0:T(4,128)(2,1)S(1)} %pad_maximum_fusion.x_ref, bf16[4,256,768]{2,1,0:T(8,128)(2,1)S(1)} %bitcast.1, s32[4,256]{1,0:T(4,128)S(1)} %copy-done, s32[4,2]{1,0:T(4,128)S(1)} %pad_add_fusion.gap_ref), custom_call_target="tpu_custom_call" | custom-call | tf_op jit(solution)/shard_map/correlate/pallas_call | solution.py:105
  50.2 0.0 reduce-scatter.2.cloned.1.call-update
  50.2 47.8 %reduce-scatter.2.cloned.1.call-done = f32[64,2048]{1,0:T(8,128)} async-done(((f32[256,2048]{1,0:T(8,128)}), f32[64,2048]{1,0:T(8,128)}) %reduce-scatter.2.cloned.1.call-update) | async-done | bytes 524304 | tf_op jit(solution)/shard_map/reduce_scatter | solution.py:131
Async XLA Ops:
  6.5 91.5 %reduce-scatter.2.cloned.1.call-start = ((), (), s32[]{:S(2)}) async-start(), calls=%async_computation.1 | async-start | bytes 2621440 | tf_op jit(solution)/shard_map/reduce_scatter | solution.py:131
  7.4 4.0 %collective-permute-start = (bf16[4,3,2048]{2,1,0:T(4,128)(2,1)S(1)}, bf16[4,3,2048]{2,1,0:T(4,128)(2,1)S(1)}, u32[]{:S(2)}, u32[]{:S(2)}) collective-permute-start(bf16[4,3,2048]{2,1,0:T(4,128)(2,1)S(1)} %copy.6), channel_id=1, source_target_pairs={{1,0},{2,1},{3,2},{4,3},{5,4},{6,5},{7,6},{9,8},{10,9},{11,10},{12... | collective-permute-start | bytes 147464 | tf_op jit(solution)/shard_map/ppermute | solution.py:25
  9.6 1.8 %copy-start = (s32[4,256]{1,0:T(4,128)S(1)}, s32[4,256]{1,0:T(4,128)}, u32[]{:S(2)}) copy-start(s32[4,256]{1,0:T(4,128)} %lag_ref.1) | copy-start | bytes 12292
Sparse Core Ops, SparseCore 0:
  50.4 47.5 reduce-scatter.1

commit v2 on v1

v2 whole, which is shorter than its diff:
```python
import functools

import jax
import jax.numpy as jnp
from jax import lax
from jax.experimental import pallas as pl
from jax.experimental.pallas import tpu as pltpu
from jax.sharding import PartitionSpec as P

TLEN = 256
MAXMOVE = 1792
BLOCK = 2048
EPSILON = 1e-06
WIN = 2 * BLOCK
COLS = BLOCK + MAXMOVE
LANES = 128
ROWS = COLS // LANES + 1
OUTR = BLOCK // LANES
TILE = 1280
LEVELS = 32767.0
MESH = pl.DeviceIdType.MESH


def left(value, amount):
    size = value.shape[-1]
    return value if amount % size == 0 else pltpu.roll(value, (-amount) % size, axis=1)


def stack_kernel(
    peers, blocks, stas, x_ref, w_ref, lag_ref, gap_ref, out_ref,
    nxt, wave, hank, scale, tscale, corr, stack, q_send, m_send, q_recv, m_recv,
    halo_sem, qs_sem, qr_sem, ms_sem, mr_sem,
):
    ntemp = w_ref.shape[1]
    mine = ntemp // peers
    groups = mine // 8
    me_sta = lax.axis_index("sta")
    me_tm = lax.axis_index("tm")
    before = lax.rem(me_tm + blocks - 1, blocks)
    after = lax.rem(me_tm + 1, blocks)
    half = peers // 2

    barrier = pltpu.get_barrier_semaphore()
    for other in (before, after):
        pl.semaphore_signal(barrier, inc=1, device_id={"tm": other}, device_id_type=MESH)
    for d in range(1, peers):
        pl.semaphore_signal(barrier, inc=1, device_id={"sta": lax.rem(me_sta + d, peers)}, device_id_type=MESH)
    pl.semaphore_wait(barrier, peers + 1)

    halo = pltpu.make_async_remote_copy(
        src_ref=x_ref, dst_ref=nxt, send_sem=halo_sem.at[0], recv_sem=halo_sem.at[1],
        device_id={"tm": before}, device_id_type=MESH,
    )
    halo.start()

    def template_scale(s, carry):
        wf = w_ref[s].astype(jnp.float32)
        te = jnp.sum(wf * wf, axis=1, keepdims=True) / (3 * TLEN)
        tscale[pl.ds(pl.multiple_of(s * ntemp, ntemp), ntemp), :] = jnp.broadcast_to(
            lax.rsqrt(te + EPSILON), (ntemp, LANES)
        )
        return carry

    lax.fori_loop(0, stas, template_scale, 0)
    halo.wait()

    present = (me_tm < blocks - 1).astype(jnp.float32)
    wave[:, :BLOCK] = x_ref[...].astype(jnp.float32)
    wave[:, BLOCK:] = nxt[...].astype(jnp.float32) * present
    squares = wave[...] * wave[...]
    run = squares[:stas] + squares[stas : 2 * stas] + squares[2 * stas : 3 * stas]
    step = 1
    while step < TLEN:
        run = run + left(run, step)
        step *= 2
    row = lax.rsqrt(run / (3 * TLEN) + EPSILON) * (1.0 / (3 * TLEN))
    lane = lax.broadcasted_iota(jnp.int32, (stas, WIN), 1)
    sub = lax.broadcasted_iota(jnp.int32, (stas, WIN), 0)
    alive = jnp.zeros((stas, WIN), jnp.int32)
    later = lax.min(me_tm + 1, blocks - 1)
    for s in range(stas):
        alive = jnp.where(sub == s, jnp.where(lane < BLOCK, gap_ref[s, me_tm], gap_ref[s, later]), alive)
    scale[...] = row * alive.astype(jnp.float32)

    sub8 = lax.broadcasted_iota(jnp.int32, (8, WIN), 0)

    def build(i, carry):
        base = jnp.broadcast_to(wave[pl.ds(i, 1), :], (8, WIN))
        for bit in (1, 2, 4):
            base = jnp.where((sub8 & bit) != 0, left(base, bit), base)
        for a in range(8):
            pair = jnp.concatenate([left(base, 16 * a), left(base, 16 * a + 8)], axis=0)
            hank[i, 16 * a : 16 * (a + 1), :] = pair.astype(jnp.bfloat16)
        return carry

    lax.fori_loop(0, 3 * stas, build, 0)

    lanes = lax.broadcasted_iota(jnp.int32, (OUTR, LANES), 1)
    wide = ntemp // 2
    corr_rows = wide * ROWS

    def correlate(side):
        first = pl.multiple_of(side * wide, wide)

        def station(s, carry):
            wt = w_ref[s, pl.ds(first, wide), :]
            ts = tscale[pl.ds(pl.multiple_of(s * ntemp + first, wide), wide), :]

            def tile(i, carry):
                start = pl.multiple_of(i * TILE, TILE)
                parts = []
                for c in range(3):
                    parts.append(hank[c * stas + s, :, pl.ds(start, TILE)])
                    parts.append(hank[c * stas + s, :, pl.ds(start + LANES, TILE)])
                rhs = jnp.concatenate(parts, axis=0)
                prod = lax.dot_general(wt, rhs, (((1,), (0,)), ((), ())), preferred_element_type=jnp.float32)
                prod = prod * scale[pl.ds(s, 1), pl.ds(start, TILE)]
                for h in range(TILE // LANES):
                    part = prod[:, LANES * h : LANES * (h + 1)] * ts
                    for g in range(wide // 8):
                        at = s * corr_rows + g * 8 * ROWS + i * (TILE // LANES) + h
                        corr[pl.ds(at, 8, stride=ROWS), :] = part[8 * g : 8 * g + 8]
                return carry

            return lax.fori_loop(0, COLS // TILE, tile, carry)

        lax.fori_loop(0, stas, station, 0)

    def shift_group(dest, g, slot):
        for k in range(8):
            total = None
            for s in range(stas):
                lag = lag_ref[s, dest * mine + g * 8 + k]
                r = lag & (LANES - 1)
                at = s * corr_rows + (lax.rem(dest, half) * mine + g * 8 + k) * ROWS + (lag >> 7)
                lo = corr[pl.ds(at, OUTR), :]
                hi = corr[pl.ds(at + 1, OUTR), :]
                term = pltpu.roll(jnp.where(lanes >= r, lo, hi), (LANES - r) & (LANES - 1), axis=1)
                total = term if total is None else total + term
            stack[pl.ds(slot * 8 * OUTR + k, OUTR, stride=8), :] = total

    def send_copies(i, dest):
        q_copy = pltpu.make_async_remote_copy(
            src_ref=q_send.at[i], dst_ref=q_recv.at[i], send_sem=qs_sem.at[i], recv_sem=qr_sem.at[i],
            device_id={"sta": dest}, device_id_type=MESH,
        )
        m_copy = pltpu.make_async_remote_copy(
            src_ref=m_send.at[i], dst_ref=m_recv.at[i], send_sem=ms_sem.at[i], recv_sem=mr_sem.at[i],
            device_id={"sta": dest}, device_id_type=MESH,
        )
        return q_copy, m_copy

    def target(i):
        side = me_sta // half
        far = (1 - side) * half + lax.rem(me_sta + i, half)
        near = side * half + lax.rem(me_sta + 1 + i, half)
        return jnp.where(i < half, far, near)

    def chunk(i, carry):
        dest = target(i)

        def pair(gp, carry):
            for h in range(2):
                shift_group(dest, gp * 2 + h, h)
            rows = pl.ds(pl.multiple_of(gp * 16, 16), 16)
            big = None
            vals = []
            for p in range(OUTR):
                v = jnp.concatenate(
                    [stack[8 * p : 8 * p + 8, :], stack[8 * OUTR + 8 * p : 8 * OUTR + 8 * p + 8, :]], axis=0
                )
                vals.append(v)
                big = jnp.abs(v) if big is None else jnp.maximum(big, jnp.abs(v))
            top = jnp.max(big, axis=1, keepdims=True) * 1.01
            top16 = jnp.broadcast_to(jnp.maximum(top, 1e-30), (16, LANES)).astype(jnp.bfloat16)
            m_send[i, rows, :] = top16
            inv = 1.0 / top16.astype(jnp.float32)
            for p in range(OUTR):
                a = jnp.abs(vals[p]) * inv
                root = a * lax.rsqrt(jnp.maximum(a, 1e-30))
                level = (root * LEVELS + 0.5).astype(jnp.int32)
                level = jnp.where(vals[p] < 0.0, -level, level)
                q_send[i, rows, LANES * p : LANES * (p + 1)] = level.astype(jnp.int16)
            return carry

        lax.fori_loop(0, groups // 2, pair, 0)
        for copy in send_copies(i, dest):
            copy.start()
        return carry

    correlate(1 - me_sta // half)
    lax.fori_loop(0, half, chunk, 0)
    correlate(me_sta // half)
    lax.fori_loop(half, peers - 1, chunk, 0)

    def own(g, carry):
        shift_group(me_sta, g, 0)
        for p in range(OUTR):
            out_ref[pl.ds(pl.multiple_of(g * 8, 8), 8), LANES * p : LANES * (p + 1)] = stack[8 * p : 8 * p + 8, :]
        return carry

    lax.fori_loop(0, groups, own, 0)

    def collect(i, carry):
        for copy in send_copies(i, target(i)):
            copy.wait()

        def add(gp, carry):
            rows = pl.ds(pl.multiple_of(gp * 16, 16), 16)
            unit = m_recv[i, rows, :].astype(jnp.float32) * (1.0 / (LEVELS * LEVELS))
            for p in range(OUTR):
                level = q_recv[i, rows, LANES * p : LANES * (p + 1)].astype(jnp.int32).astype(jnp.float32)
                out_ref[rows, LANES * p : LANES * (p + 1)] += level * jnp.abs(level) * unit
            return carry

        return lax.fori_loop(0, mine // 16, add, carry)

    lax.fori_loop(0, peers - 1, collect, 0)


def local(waveforms, templates, moveouts, gap_masks):
    stas, _, block = waveforms.shape
    ntemp = templates.shape[2]
    peers, blocks = lax.axis_size("sta"), lax.axis_size("tm")
    mine = ntemp // peers
    lines = -(-3 * stas // 16) * 16
    x = jnp.transpose(waveforms, (1, 0, 2)).reshape(3 * stas, block)
    x = jnp.pad(x, ((0, lines - 3 * stas), (0, 0)))
    wt = jnp.transpose(templates, (0, 2, 1))
    vmem = pl.BlockSpec(memory_space=pltpu.VMEM)
    smem = pl.BlockSpec(memory_space=pltpu.SMEM)
    dma = pltpu.SemaphoreType.DMA((peers - 1,))
    return pl.pallas_call(
        functools.partial(stack_kernel, peers, blocks, stas),
        out_shape=jax.ShapeDtypeStruct((mine, BLOCK), jnp.float32),
        in_specs=[vmem, vmem, smem, smem],
        out_specs=vmem,
        scratch_shapes=[
            pltpu.VMEM((lines, BLOCK), jnp.bfloat16),
            pltpu.VMEM((lines, WIN), jnp.float32),
            pltpu.VMEM((3 * stas, LANES, WIN), jnp.bfloat16),
            pltpu.VMEM((stas, WIN), jnp.float32),
            pltpu.VMEM((stas * ntemp, LANES), jnp.float32),
            pltpu.VMEM((stas * (ntemp // 2) * ROWS, LANES), jnp.float32),
            pltpu.VMEM((2 * OUTR * 8, LANES), jnp.float32),
            pltpu.VMEM((peers - 1, mine, BLOCK), jnp.int16),
            pltpu.VMEM((peers - 1, mine, LANES), jnp.bfloat16),
            pltpu.VMEM((peers - 1, mine, BLOCK), jnp.int16),
            pltpu.VMEM((peers - 1, mine, LANES), jnp.bfloat16),
            pltpu.SemaphoreType.DMA((2,)),
            dma, dma, dma, dma,
        ],
        compiler_params=pltpu.CompilerParams(
            collective_id=0, has_side_effects=True, vmem_limit_bytes=48 * 1024 * 1024
        ),
        name="stack",
    )(x, wt, moveouts, gap_masks)


def solution(mesh):
    in_specs = (P("sta", None, "tm"), P("sta", None, None), P("sta", None), P("sta", None))
    out_specs = P("sta", "tm")
    return jax.shard_map(local, mesh=mesh, in_specs=in_specs, out_specs=out_specs, check_vma=False)
```

time: 105 us -> 52.3 us (0.50)
  waiting for transfers between devices: 47.8 us -> 0 us
  between operations: 13.4 us -> 0.06 us
  Pallas kernels: 38.8 us -> 48.7 us
  starting transfers between devices: 1.29 us -> 0 us
    reduce_scatter x1 -> x0, waiting for transfers between devices: 47.8 us -> none  [local(): return lax.psum_scatter(stacked, 'sta', scatter_dimension=0, tiled=True)]
    pallas_call x1, Pallas kernels: 38.8 us -> 48.7 us  [local(): pl.pallas_call(functools.partial(stack_kernel, peers, blocks, stas), out_...]
    ppermute x1 -> x0, starting transfers between devices: 1.29 us -> none  [shifted(): return lax.ppermute(block, axis, route)]
    unnamed x4 -> x6, local copies, waits for them, and re-layouts: 2.57 us -> 2.53 us
  transfers between devices with their start and end apart: 2 -> 0, of which waited for: 1 -> 0; matrix products, arithmetic and copies ran while one was open for 3% -> 0% of each run, Pallas kernels for 0% -> 0%
where the time goes in v2:
time: 52.3 us; the launch traced here: 52.1 us
  Pallas kernels  48.7 us (93%)
  local copies, waits for them, and re-layouts  3.35 us (6%)
    pallas_call x1, Pallas kernels, local(): pl.pallas_call(functools.partial(stack_kernel, peers, blocks, stas), out_...  48.7 us
    unnamed x6, local copies, waits for them, and re-layouts  2.53 us

profile of v2, /device:TPU:0, one launch (start us, length us, event | category | flops | bytes accessed | tf_op | source)
XLA Modules:
  0.0 52.1 jit_solution(9622874240562944516)
XLA Ops:
  0.0 0.8 %reshape.3 = bf16[12,2048]{1,0:T(8,128)(2,1)S(1)} reshape(bf16[3,4,2048]{2,1,0:T(4,128)(2,1)} %bitcast.3) | data formatting | bytes 98304 | tf_op jit(solution)/shard_map/reshape | solution.py:227
  0.8 0.0 copy-start
  0.8 0.0 copy-start.1
  0.9 1.7 %copy.5 = bf16[4,768,256]{1,2,0:T(8,128)(2,1)S(1)} copy(bf16[4,768,256]{2,1,0:T(8,128)(2,1)} %param.5) | data formatting | bytes 3145728 | tf_op args[1]
  2.6 0.0 copy-done
  2.6 0.0 copy-done.1
  2.6 48.7 %stack.1 = f32[64,2048]{1,0:T(8,128)S(1)} custom-call(bf16[16,2048]{1,0:T(8,128)(2,1)S(1)} %pad.4.x_ref, bf16[4,256,768]{2,1,0:T(8,128)(2,1)S(1)} %bitcast.2, s32[4,256]{1,0:T(4,128)S(1)} %copy-done, s32[4,8]{1,0:T(4,128)S(1)} %copy-done.1), custom_call_target="tpu_custom_call" | custom-call | tf_op jit(solution)/shard_map/stack/pallas_call | solution.py:233
  51.3 0.8 %copy.7 = f32[64,2048]{1,0:T(8,128)} copy(f32[64,2048]{1,0:T(8,128)S(1)} %stack.1) | data formatting | bytes 1048576
  (1 shorter events, 0.0 us)
Async XLA Ops:
  0.8 1.8 %copy-start = (s32[4,256]{1,0:T(4,128)S(1)}, s32[4,256]{1,0:T(4,128)}, u32[]{:S(2)}) copy-start(s32[4,256]{1,0:T(4,128)} %lag_ref.1) | copy-start | bytes 12292
  0.8 1.8 %copy-start.1 = (s32[4,8]{1,0:T(4,128)S(1)}, s32[4,8]{1,0:T(4,128)}, u32[]{:S(2)}) copy-start(s32[4,8]{1,0:T(4,128)} %gap_ref.1) | copy-start | bytes 388

commit v3 on v2

--- a/solution.py
+++ b/solution.py
@@ -28,10 +28,10 @@
 
 def stack_kernel(
     peers, blocks, stas, x_ref, w_ref, lag_ref, gap_ref, out_ref,
-    nxt, wave, hank, scale, tscale, corr, stack, q_send, m_send, q_recv, m_recv,
+    x_mine, nxt, wt_all, wave, hank, scale, tscale, corr, stack, q_send, m_send, q_recv, m_recv,
     halo_sem, qs_sem, qr_sem, ms_sem, mr_sem,
 ):
-    ntemp = w_ref.shape[1]
+    ntemp = w_ref.shape[2]
     mine = ntemp // peers
     groups = mine // 8
     me_sta = lax.axis_index("sta")
@@ -45,30 +45,52 @@
         pl.semaphore_signal(barrier, inc=1, device_id={"tm": other}, device_id_type=MESH)
     for d in range(1, peers):
         pl.semaphore_signal(barrier, inc=1, device_id={"sta": lax.rem(me_sta + d, peers)}, device_id_type=MESH)
+    lines = x_mine.shape[0]
+    records = [x_ref[s] for s in range(stas)] + [jnp.zeros((lines - 3 * stas, BLOCK), jnp.bfloat16)]
+    wave[:, :BLOCK] = jnp.concatenate([part.astype(jnp.float32) for part in records], axis=0)
+    x_mine[...] = wave[:, :BLOCK].astype(jnp.bfloat16)
     pl.semaphore_wait(barrier, peers + 1)
 
     halo = pltpu.make_async_remote_copy(
-        src_ref=x_ref, dst_ref=nxt, send_sem=halo_sem.at[0], recv_sem=halo_sem.at[1],
+        src_ref=x_mine, dst_ref=nxt, send_sem=halo_sem.at[0], recv_sem=halo_sem.at[1],
         device_id={"tm": before}, device_id_type=MESH,
     )
     halo.start()
 
     def template_scale(s, carry):
         wf = w_ref[s].astype(jnp.float32)
-        te = jnp.sum(wf * wf, axis=1, keepdims=True) / (3 * TLEN)
-        tscale[pl.ds(pl.multiple_of(s * ntemp, ntemp), ntemp), :] = jnp.broadcast_to(
-            lax.rsqrt(te + EPSILON), (ntemp, LANES)
-        )
+        te = jnp.sum(wf * wf, axis=0, keepdims=True) / (3 * TLEN)
+        across = jnp.broadcast_to(lax.rsqrt(te + EPSILON), (LANES, ntemp))
+        tscale[pl.ds(pl.multiple_of(s * ntemp, ntemp), ntemp), :] = jnp.transpose(across)
+        wt_all[s] = jnp.transpose(w_ref[s])
         return carry
 
     lax.fori_loop(0, stas, template_scale, 0)
+
+    def build(start, size, keep):
+        sub8 = lax.broadcasted_iota(jnp.int32, (8, size), 0)
+
+        def line(i, carry):
+            base = jnp.broadcast_to(wave[pl.ds(i, 1), start : start + size], (8, size))
+            for bit in (1, 2, 4):
+                base = jnp.where((sub8 & bit) != 0, left(base, bit), base)
+            for a in range(8):
+                pair = jnp.concatenate([left(base, 16 * a), left(base, 16 * a + 8)], axis=0)
+                hank[i, 16 * a : 16 * (a + 1), start : start + keep] = pair[:, :keep].astype(jnp.bfloat16)
+            return carry
+
+        lax.fori_loop(0, 3 * stas, line, 0)
+
+    build(0, BLOCK, BLOCK - LANES)
     halo.wait()
 
     present = (me_tm < blocks - 1).astype(jnp.float32)
-    wave[:, :BLOCK] = x_ref[...].astype(jnp.float32)
     wave[:, BLOCK:] = nxt[...].astype(jnp.float32) * present
     squares = wave[...] * wave[...]
-    run = squares[:stas] + squares[stas : 2 * stas] + squares[2 * stas : 3 * stas]
+    run = jnp.concatenate(
+        [squares[3 * s : 3 * s + 1] + squares[3 * s + 1 : 3 * s + 2] + squares[3 * s + 2 : 3 * s + 3] for s in range(stas)],
+        axis=0,
+    )
     step = 1
     while step < TLEN:
         run = run + left(run, step)
@@ -81,19 +103,7 @@
     for s in range(stas):
         alive = jnp.where(sub == s, jnp.where(lane < BLOCK, gap_ref[s, me_tm], gap_ref[s, later]), alive)
     scale[...] = row * alive.astype(jnp.float32)
-
-    sub8 = lax.broadcasted_iota(jnp.int32, (8, WIN), 0)
-
-    def build(i, carry):
-        base = jnp.broadcast_to(wave[pl.ds(i, 1), :], (8, WIN))
-        for bit in (1, 2, 4):
-            base = jnp.where((sub8 & bit) != 0, left(base, bit), base)
-        for a in range(8):
-            pair = jnp.concatenate([left(base, 16 * a), left(base, 16 * a + 8)], axis=0)
-            hank[i, 16 * a : 16 * (a + 1), :] = pair.astype(jnp.bfloat16)
-        return carry
-
-    lax.fori_loop(0, 3 * stas, build, 0)
+    build(BLOCK - LANES, BLOCK + LANES, BLOCK + LANES)
 
     lanes = lax.broadcasted_iota(jnp.int32, (OUTR, LANES), 1)
     wide = ntemp // 2
@@ -103,15 +113,15 @@
         first = pl.multiple_of(side * wide, wide)
 
         def station(s, carry):
-            wt = w_ref[s, pl.ds(first, wide), :]
+            wt = wt_all[s, pl.ds(first, wide), :]
             ts = tscale[pl.ds(pl.multiple_of(s * ntemp + first, wide), wide), :]
 
             def tile(i, carry):
                 start = pl.multiple_of(i * TILE, TILE)
                 parts = []
                 for c in range(3):
-                    parts.append(hank[c * stas + s, :, pl.ds(start, TILE)])
-                    parts.append(hank[c * stas + s, :, pl.ds(start + LANES, TILE)])
+                    parts.append(hank[3 * s + c, :, pl.ds(start, TILE)])
+                    parts.append(hank[3 * s + c, :, pl.ds(start + LANES, TILE)])
                 rhs = jnp.concatenate(parts, axis=0)
                 prod = lax.dot_general(wt, rhs, (((1,), (0,)), ((), ())), preferred_element_type=jnp.float32)
                 prod = prod * scale[pl.ds(s, 1), pl.ds(start, TILE)]
@@ -159,7 +169,9 @@
     def chunk(i, carry):
         dest = target(i)
 
-        def pair(gp, carry):
+        lane16 = lax.broadcasted_iota(jnp.int32, (16, LANES), 1)
+
+        def pair(gp, tops):
             for h in range(2):
                 shift_group(dest, gp * 2 + h, h)
             rows = pl.ds(pl.multiple_of(gp * 16, 16), 16)
@@ -173,17 +185,18 @@
                 big = jnp.abs(v) if big is None else jnp.maximum(big, jnp.abs(v))
             top = jnp.max(big, axis=1, keepdims=True) * 1.01
             top16 = jnp.broadcast_to(jnp.maximum(top, 1e-30), (16, LANES)).astype(jnp.bfloat16)
-            m_send[i, rows, :] = top16
-            inv = 1.0 / top16.astype(jnp.float32)
+            top32 = top16.astype(jnp.float32)
+            inv = 1.0 / top32
             for p in range(OUTR):
                 a = jnp.abs(vals[p]) * inv
                 root = a * lax.rsqrt(jnp.maximum(a, 1e-30))
                 level = (root * LEVELS + 0.5).astype(jnp.int32)
                 level = jnp.where(vals[p] < 0.0, -level, level)
                 q_send[i, rows, LANES * p : LANES * (p + 1)] = level.astype(jnp.int16)
-            return carry
-
-        lax.fori_loop(0, groups // 2, pair, 0)
+            return jnp.where(lane16 == gp, top32, tops)
+
+        tops = lax.fori_loop(0, groups // 2, pair, jnp.zeros((16, LANES), jnp.float32))
+        m_send[i] = tops.astype(jnp.bfloat16)
         for copy in send_copies(i, dest):
             copy.start()
         return carry
@@ -207,7 +220,9 @@
 
         def add(gp, carry):
             rows = pl.ds(pl.multiple_of(gp * 16, 16), 16)
-            unit = m_recv[i, rows, :].astype(jnp.float32) * (1.0 / (LEVELS * LEVELS))
+            lane16 = lax.broadcasted_iota(jnp.int32, (16, LANES), 1)
+            tops = jnp.where(lane16 == gp, m_recv[i].astype(jnp.float32), 0.0)
+            unit = jnp.sum(tops, axis=1, keepdims=True) * (1.0 / (LEVELS * LEVELS))
             for p in range(OUTR):
                 level = q_recv[i, rows, LANES * p : LANES * (p + 1)].astype(jnp.int32).astype(jnp.float32)
                 out_ref[rows, LANES * p : LANES * (p + 1)] += level * jnp.abs(level) * unit
@@ -219,14 +234,11 @@
 
 
 def local(waveforms, templates, moveouts, gap_masks):
-    stas, _, block = waveforms.shape
+    stas = waveforms.shape[0]
     ntemp = templates.shape[2]
     peers, blocks = lax.axis_size("sta"), lax.axis_size("tm")
     mine = ntemp // peers
     lines = -(-3 * stas // 16) * 16
-    x = jnp.transpose(waveforms, (1, 0, 2)).reshape(3 * stas, block)
-    x = jnp.pad(x, ((0, lines - 3 * stas), (0, 0)))
-    wt = jnp.transpose(templates, (0, 2, 1))
     vmem = pl.BlockSpec(memory_space=pltpu.VMEM)
     smem = pl.BlockSpec(memory_space=pltpu.SMEM)
     dma = pltpu.SemaphoreType.DMA((peers - 1,))
@@ -237,6 +249,8 @@
         out_specs=vmem,
         scratch_shapes=[
             pltpu.VMEM((lines, BLOCK), jnp.bfloat16),
+            pltpu.VMEM((lines, BLOCK), jnp.bfloat16),
+            pltpu.VMEM((stas, ntemp, 3 * TLEN), jnp.bfloat16),
             pltpu.VMEM((lines, WIN), jnp.float32),
             pltpu.VMEM((3 * stas, LANES, WIN), jnp.bfloat16),
             pltpu.VMEM((stas, WIN), jnp.float32),
@@ -244,9 +258,9 @@
             pltpu.VMEM((stas * (ntemp // 2) * ROWS, LANES), jnp.float32),
             pltpu.VMEM((2 * OUTR * 8, LANES), jnp.float32),
             pltpu.VMEM((peers - 1, mine, BLOCK), jnp.int16),
-            pltpu.VMEM((peers - 1, mine, LANES), jnp.bfloat16),
+            pltpu.VMEM((peers - 1, 16, LANES), jnp.bfloat16),
             pltpu.VMEM((peers - 1, mine, BLOCK), jnp.int16),
-            pltpu.VMEM((peers - 1, mine, LANES), jnp.bfloat16),
+            pltpu.VMEM((peers - 1, 16, LANES), jnp.bfloat16),
             pltpu.SemaphoreType.DMA((2,)),
             dma, dma, dma, dma,
         ],
@@ -254,7 +268,7 @@
             collective_id=0, has_side_effects=True, vmem_limit_bytes=48 * 1024 * 1024
         ),
         name="stack",
-    )(x, wt, moveouts, gap_masks)
+    )(waveforms, templates, moveouts, gap_masks)
 
 
 def solution(mesh):

time: 52.3 us -> 54.2 us (1.036)
  local copies, waits for them, and re-layouts: 3.35 us -> 4.41 us
  Pallas kernels: 48.7 us -> 49.6 us
    unnamed x6 -> x8, local copies, waits for them, and re-layouts: 2.53 us -> 4.41 us
    pallas_call x1, Pallas kernels: 48.7 us -> 49.6 us  [local(): pl.pallas_call(functools.partial(stack_kernel, peers, blocks, stas), out_...]
    reshape x1 -> x0, local copies, waits for them, and re-layouts: 0.82 us -> none  [local(): x = jnp.transpose(waveforms, (1, 0, 2)).reshape(3 * stas, block)]
where the time goes in v3:
time: 54.2 us; the launch traced here: 54 us
  Pallas kernels  49.6 us (92%)
  local copies, waits for them, and re-layouts  4.41 us (8%)
    pallas_call x1, Pallas kernels, local(): pl.pallas_call(functools.partial(stack_kernel, peers, blocks, stas), out_...  49.6 us
    unnamed x8, local copies, waits for them, and re-layouts  4.41 us

profile of v3, /device:TPU:0, one launch (start us, length us, event | category | flops | bytes accessed | tf_op | source)
XLA Modules:
  0.0 54.0 jit_solution(8336133530744323055)
XLA Ops:
  0.0 0.8 %copy.5.x_ref = bf16[4,3,2048]{2,1,0:T(4,128)(2,1)S(1)} copy(bf16[4,3,2048]{2,0,1:T(4,128)(2,1)} %param.4) | data formatting | bytes 98304 | tf_op args[0]
  0.8 0.0 copy-start
  0.9 1.4 %copy-done = bf16[4,768,256]{2,1,0:T(8,128)(2,1)S(1)} copy-done((bf16[4,768,256]{2,1,0:T(8,128)(2,1)S(1)}, bf16[4,768,256]{2,1,0:T(8,128)(2,1)}, u32[]{:S(2)}) %copy-start) | copy-done | bytes 1572888
  2.3 0.0 copy-start.1
  2.3 0.7 %copy-done.1 = s32[4,256]{1,0:T(4,128)S(1)} copy-done((s32[4,256]{1,0:T(4,128)S(1)}, s32[4,256]{1,0:T(4,128)}, u32[]{:S(2)}) %copy-start.1) | copy-done | bytes 4120
  2.9 0.0 copy-start.2
  2.9 0.7 %copy-done.2 = s32[4,8]{1,0:T(4,128)S(1)} copy-done((s32[4,8]{1,0:T(4,128)S(1)}, s32[4,8]{1,0:T(4,128)}, u32[]{:S(2)}) %copy-start.2) | copy-done | bytes 152
  3.6 49.6 %stack.1 = f32[64,2048]{1,0:T(8,128)S(1)} custom-call(bf16[4,3,2048]{2,1,0:T(4,128)(2,1)S(1)} %copy.5.x_ref, bf16[4,768,256]{2,1,0:T(8,128)(2,1)S(1)} %copy-done, s32[4,256]{1,0:T(4,128)S(1)} %copy-done.1, s32[4,8]{1,0:T(4,128)S(1)} %copy-done.2), custom_call_target="tpu_custom_call" | custom-call | tf_op jit(solution)/shard_map/stack/pallas_call | solution.py:245
  53.2 0.8 %copy.7 = f32[64,2048]{1,0:T(8,128)} copy(f32[64,2048]{1,0:T(8,128)S(1)} %stack.1) | data formatting | bytes 1048576
Async XLA Ops:
  0.8 1.4 %copy-start = (bf16[4,768,256]{2,1,0:T(8,128)(2,1)S(1)}, bf16[4,768,256]{2,1,0:T(8,128)(2,1)}, u32[]{:S(2)}) copy-start(bf16[4,768,256]{2,1,0:T(8,128)(2,1)} %w_ref.1) | copy-start | bytes 4718596
  2.3 0.7 %copy-start.1 = (s32[4,256]{1,0:T(4,128)S(1)}, s32[4,256]{1,0:T(4,128)}, u32[]{:S(2)}) copy-start(s32[4,256]{1,0:T(4,128)} %lag_ref.1) | copy-start | bytes 12292
  2.9 0.7 %copy-start.2 = (s32[4,8]{1,0:T(4,128)S(1)}, s32[4,8]{1,0:T(4,128)}, u32[]{:S(2)}) copy-start(s32[4,8]{1,0:T(4,128)} %gap_ref.1) | copy-start | bytes 388

commit v4 on v3

--- a/solution.py
+++ b/solution.py
@@ -27,9 +27,9 @@
 
 
 def stack_kernel(
-    peers, blocks, stas, x_ref, w_ref, lag_ref, gap_ref, out_ref,
-    x_mine, nxt, wt_all, wave, hank, scale, tscale, corr, stack, q_send, m_send, q_recv, m_recv,
-    halo_sem, qs_sem, qr_sem, ms_sem, mr_sem,
+    peers, blocks, stas, x_ref, w_hbm, lag_hbm, gap_hbm, out_ref,
+    w_ref, lag_ref, gap_ref, x_mine, nxt, wt_all, wave, hank, scale, tscale, corr, stack, q_send, m_send, q_recv, m_recv,
+    load_sem, halo_sem, qs_sem, qr_sem, ms_sem, mr_sem,
 ):
     ntemp = w_ref.shape[2]
     mine = ntemp // peers
@@ -40,13 +40,20 @@
     after = lax.rem(me_tm + 1, blocks)
     half = peers // 2
 
+    loads = [
+        pltpu.make_async_copy(w_hbm, w_ref, load_sem.at[0]),
+        pltpu.make_async_copy(lag_hbm, lag_ref, load_sem.at[1]),
+        pltpu.make_async_copy(gap_hbm, gap_ref, load_sem.at[2]),
+    ]
+    for load in loads:
+        load.start()
     barrier = pltpu.get_barrier_semaphore()
     for other in (before, after):
         pl.semaphore_signal(barrier, inc=1, device_id={"tm": other}, device_id_type=MESH)
     for d in range(1, peers):
         pl.semaphore_signal(barrier, inc=1, device_id={"sta": lax.rem(me_sta + d, peers)}, device_id_type=MESH)
     lines = x_mine.shape[0]
-    records = [x_ref[s] for s in range(stas)] + [jnp.zeros((lines - 3 * stas, BLOCK), jnp.bfloat16)]
+    records = [x_ref[c] for c in range(3)] + [jnp.zeros((lines - 3 * stas, BLOCK), jnp.bfloat16)]
     wave[:, :BLOCK] = jnp.concatenate([part.astype(jnp.float32) for part in records], axis=0)
     x_mine[...] = wave[:, :BLOCK].astype(jnp.bfloat16)
     pl.semaphore_wait(barrier, peers + 1)
@@ -57,15 +64,21 @@
     )
     halo.start()
 
-    def template_scale(s, carry):
-        wf = w_ref[s].astype(jnp.float32)
-        te = jnp.sum(wf * wf, axis=0, keepdims=True) / (3 * TLEN)
-        across = jnp.broadcast_to(lax.rsqrt(te + EPSILON), (LANES, ntemp))
-        tscale[pl.ds(pl.multiple_of(s * ntemp, ntemp), ntemp), :] = jnp.transpose(across)
-        wt_all[s] = jnp.transpose(w_ref[s])
-        return carry
-
-    lax.fori_loop(0, stas, template_scale, 0)
+    wide = ntemp // 2
+
+    def prepare(side):
+        first = pl.multiple_of(side * wide, wide)
+
+        def template_scale(s, carry):
+            w = w_ref[s, :, pl.ds(first, wide)]
+            wf = w.astype(jnp.float32)
+            te = jnp.sum(wf * wf, axis=0, keepdims=True) / (3 * TLEN)
+            across = jnp.broadcast_to(lax.rsqrt(te + EPSILON), (LANES, wide))
+            tscale[pl.ds(pl.multiple_of(s * wide, wide), wide), :] = jnp.transpose(across)
+            wt_all[s] = jnp.transpose(w)
+            return carry
+
+        lax.fori_loop(0, stas, template_scale, 0)
 
     def build(start, size, keep):
         sub8 = lax.broadcasted_iota(jnp.int32, (8, size), 0)
@@ -82,15 +95,15 @@
         lax.fori_loop(0, 3 * stas, line, 0)
 
     build(0, BLOCK, BLOCK - LANES)
+    for load in loads:
+        load.wait()
+    prepare(1 - me_sta // half)
     halo.wait()
 
     present = (me_tm < blocks - 1).astype(jnp.float32)
     wave[:, BLOCK:] = nxt[...].astype(jnp.float32) * present
     squares = wave[...] * wave[...]
-    run = jnp.concatenate(
-        [squares[3 * s : 3 * s + 1] + squares[3 * s + 1 : 3 * s + 2] + squares[3 * s + 2 : 3 * s + 3] for s in range(stas)],
-        axis=0,
-    )
+    run = squares[:stas] + squares[stas : 2 * stas] + squares[2 * stas : 3 * stas]
     step = 1
     while step < TLEN:
         run = run + left(run, step)
@@ -106,22 +119,19 @@
     build(BLOCK - LANES, BLOCK + LANES, BLOCK + LANES)
 
     lanes = lax.broadcasted_iota(jnp.int32, (OUTR, LANES), 1)
-    wide = ntemp // 2
     corr_rows = wide * ROWS
 
-    def correlate(side):
-        first = pl.multiple_of(side * wide, wide)
-
+    def correlate():
         def station(s, carry):
-            wt = wt_all[s, pl.ds(first, wide), :]
-            ts = tscale[pl.ds(pl.multiple_of(s * ntemp + first, wide), wide), :]
+            wt = wt_all[s]
+            ts = tscale[pl.ds(pl.multiple_of(s * wide, wide), wide), :]
 
             def tile(i, carry):
                 start = pl.multiple_of(i * TILE, TILE)
                 parts = []
                 for c in range(3):
-                    parts.append(hank[3 * s + c, :, pl.ds(start, TILE)])
-                    parts.append(hank[3 * s + c, :, pl.ds(start + LANES, TILE)])
+                    parts.append(hank[c * stas + s, :, pl.ds(start, TILE)])
+                    parts.append(hank[c * stas + s, :, pl.ds(start + LANES, TILE)])
                 rhs = jnp.concatenate(parts, axis=0)
                 prod = lax.dot_general(wt, rhs, (((1,), (0,)), ((), ())), preferred_element_type=jnp.float32)
                 prod = prod * scale[pl.ds(s, 1), pl.ds(start, TILE)]
@@ -201,9 +211,10 @@
             copy.start()
         return carry
 
-    correlate(1 - me_sta // half)
+    correlate()
     lax.fori_loop(0, half, chunk, 0)
-    correlate(me_sta // half)
+    prepare(me_sta // half)
+    correlate()
     lax.fori_loop(half, peers - 1, chunk, 0)
 
     def own(g, carry):
@@ -240,35 +251,39 @@
     mine = ntemp // peers
     lines = -(-3 * stas // 16) * 16
     vmem = pl.BlockSpec(memory_space=pltpu.VMEM)
-    smem = pl.BlockSpec(memory_space=pltpu.SMEM)
+    hbm = pl.BlockSpec(memory_space=pltpu.HBM)
     dma = pltpu.SemaphoreType.DMA((peers - 1,))
     return pl.pallas_call(
         functools.partial(stack_kernel, peers, blocks, stas),
         out_shape=jax.ShapeDtypeStruct((mine, BLOCK), jnp.float32),
-        in_specs=[vmem, vmem, smem, smem],
+        in_specs=[vmem, hbm, hbm, hbm],
         out_specs=vmem,
         scratch_shapes=[
+            pltpu.VMEM(templates.shape, jnp.bfloat16),
+            pltpu.SMEM(moveouts.shape, jnp.int32),
+            pltpu.SMEM(gap_masks.shape, jnp.int32),
             pltpu.VMEM((lines, BLOCK), jnp.bfloat16),
             pltpu.VMEM((lines, BLOCK), jnp.bfloat16),
-            pltpu.VMEM((stas, ntemp, 3 * TLEN), jnp.bfloat16),
+            pltpu.VMEM((stas, ntemp // 2, 3 * TLEN), jnp.bfloat16),
             pltpu.VMEM((lines, WIN), jnp.float32),
             pltpu.VMEM((3 * stas, LANES, WIN), jnp.bfloat16),
             pltpu.VMEM((stas, WIN), jnp.float32),
-            pltpu.VMEM((stas * ntemp, LANES), jnp.float32),
+            pltpu.VMEM((stas * (ntemp // 2), LANES), jnp.float32),
             pltpu.VMEM((stas * (ntemp // 2) * ROWS, LANES), jnp.float32),
             pltpu.VMEM((2 * OUTR * 8, LANES), jnp.float32),
             pltpu.VMEM((peers - 1, mine, BLOCK), jnp.int16),
             pltpu.VMEM((peers - 1, 16, LANES), jnp.bfloat16),
             pltpu.VMEM((peers - 1, mine, BLOCK), jnp.int16),
             pltpu.VMEM((peers - 1, 16, LANES), jnp.bfloat16),
+            pltpu.SemaphoreType.DMA((3,)),
             pltpu.SemaphoreType.DMA((2,)),
             dma, dma, dma, dma,
         ],
         compiler_params=pltpu.CompilerParams(
-            collective_id=0, has_side_effects=True, vmem_limit_bytes=48 * 1024 * 1024
+            collective_id=0, has_side_effects=True, vmem_limit_bytes=63 * 1024 * 1024 + 512 * 1024
         ),
         name="stack",
-    )(waveforms, templates, moveouts, gap_masks)
+    )(jnp.transpose(waveforms, (1, 0, 2)), templates, moveouts, gap_masks)
 
 
 def solution(mesh):

time: 54.2 us -> 52.7 us (0.972)
  local copies, waits for them, and re-layouts: 4.41 us -> 1.87 us
  Pallas kernels: 49.6 us -> 50.6 us
    unnamed x8 -> x1, local copies, waits for them, and re-layouts: 4.41 us -> 1.87 us
    pallas_call x1, Pallas kernels: 49.6 us -> 50.6 us  [local(): pl.pallas_call(functools.partial(stack_kernel, peers, blocks, stas), out_...]
where the time goes in v4:
time: 52.7 us; the launch traced here: 52.5 us
  Pallas kernels  50.6 us (96%)
  local copies, waits for them, and re-layouts  1.87 us (4%)
    pallas_call x1, Pallas kernels, local(): pl.pallas_call(functools.partial(stack_kernel, peers, blocks, stas), out_...  50.6 us
    unnamed x1, local copies, waits for them, and re-layouts  1.87 us

profile of v4, /device:TPU:0, one launch (start us, length us, event | category | flops | bytes accessed | tf_op | source)
XLA Modules:
  0.0 52.5 jit_solution(11504079015346716718)
XLA Ops:
  0.0 50.6 %stack.1 = f32[64,2048]{1,0:T(8,128)} custom-call(bf16[3,4,2048]{2,1,0:T(4,128)(2,1)} %bitcast.1, bf16[4,768,256]{2,1,0:T(8,128)(2,1)} %w_hbm.1, s32[4,256]{1,0:T(4,128)} %lag_hbm.1, s32[4,8]{1,0:T(4,128)} %gap_hbm.1), custom_call_target="tpu_custom_call" | custom-call | tf_op jit(solution)/shard_map/stack/pallas_call | solution.py:256
  50.6 1.9 %copy.6 = f32[64,2048]{1,0:T(8,128)} copy(f32[64,2048]{1,0:T(8,128)} %stack.1) | data formatting | bytes 1048576

commit v5 on v4

--- a/solution.py
+++ b/solution.py
@@ -159,16 +159,19 @@
                 total = term if total is None else total + term
             stack[pl.ds(slot * 8 * OUTR + k, OUTR, stride=8), :] = total
 
-    def send_copies(i, dest):
-        q_copy = pltpu.make_async_remote_copy(
-            src_ref=q_send.at[i], dst_ref=q_recv.at[i], send_sem=qs_sem.at[i], recv_sem=qr_sem.at[i],
+    def rows_copy(i, gp, dest):
+        rows = pl.ds(pl.multiple_of(gp * 16, 16), 16)
+        return pltpu.make_async_remote_copy(
+            src_ref=q_send.at[i, rows], dst_ref=q_recv.at[i, rows],
+            send_sem=qs_sem.at[i, gp], recv_sem=qr_sem.at[i, gp],
             device_id={"sta": dest}, device_id_type=MESH,
         )
-        m_copy = pltpu.make_async_remote_copy(
+
+    def scale_copy(i, dest):
+        return pltpu.make_async_remote_copy(
             src_ref=m_send.at[i], dst_ref=m_recv.at[i], send_sem=ms_sem.at[i], recv_sem=mr_sem.at[i],
             device_id={"sta": dest}, device_id_type=MESH,
         )
-        return q_copy, m_copy
 
     def target(i):
         side = me_sta // half
@@ -203,12 +206,12 @@
                 level = (root * LEVELS + 0.5).astype(jnp.int32)
                 level = jnp.where(vals[p] < 0.0, -level, level)
                 q_send[i, rows, LANES * p : LANES * (p + 1)] = level.astype(jnp.int16)
+            rows_copy(i, gp, dest).start()
             return jnp.where(lane16 == gp, top32, tops)
 
         tops = lax.fori_loop(0, groups // 2, pair, jnp.zeros((16, LANES), jnp.float32))
         m_send[i] = tops.astype(jnp.bfloat16)
-        for copy in send_copies(i, dest):
-            copy.start()
+        scale_copy(i, dest).start()
         return carry
 
     correlate()
@@ -226,10 +229,10 @@
     lax.fori_loop(0, groups, own, 0)
 
     def collect(i, carry):
-        for copy in send_copies(i, target(i)):
-            copy.wait()
+        scale_copy(i, target(i)).wait()
 
         def add(gp, carry):
+            rows_copy(i, gp, target(i)).wait()
             rows = pl.ds(pl.multiple_of(gp * 16, 16), 16)
             lane16 = lax.broadcasted_iota(jnp.int32, (16, LANES), 1)
             tops = jnp.where(lane16 == gp, m_recv[i].astype(jnp.float32), 0.0)
@@ -253,6 +256,7 @@
     vmem = pl.BlockSpec(memory_space=pltpu.VMEM)
     hbm = pl.BlockSpec(memory_space=pltpu.HBM)
     dma = pltpu.SemaphoreType.DMA((peers - 1,))
+    many = pltpu.SemaphoreType.DMA((peers - 1, mine // 16))
     return pl.pallas_call(
         functools.partial(stack_kernel, peers, blocks, stas),
         out_shape=jax.ShapeDtypeStruct((mine, BLOCK), jnp.float32),
@@ -277,7 +281,7 @@
             pltpu.VMEM((peers - 1, 16, LANES), jnp.bfloat16),
             pltpu.SemaphoreType.DMA((3,)),
             pltpu.SemaphoreType.DMA((2,)),
-            dma, dma, dma, dma,
+            many, many, dma, dma,
         ],
         compiler_params=pltpu.CompilerParams(
             collective_id=0, has_side_effects=True, vmem_limit_bytes=63 * 1024 * 1024 + 512 * 1024

time: 52.7 us -> 51.4 us (0.975)
  Pallas kernels: 50.6 us -> 49.3 us
    pallas_call x1, Pallas kernels: 50.6 us -> 49.3 us  [local(): pl.pallas_call(functools.partial(stack_kernel, peers, blocks, stas), out_...]
where the time goes in v5:
time: 51.4 us; the launch traced here: 51.2 us
  Pallas kernels  49.3 us (96%)
  local copies, waits for them, and re-layouts  1.87 us (4%)
    pallas_call x1, Pallas kernels, local(): pl.pallas_call(functools.partial(stack_kernel, peers, blocks, stas), out_...  49.3 us
    unnamed x1, local copies, waits for them, and re-layouts  1.87 us

profile of v5, /device:TPU:0, one launch (start us, length us, event | category | flops | bytes accessed | tf_op | source)
XLA Modules:
  0.0 51.2 jit_solution(7957762496676747711)
XLA Ops:
  0.0 49.3 %stack.1 = f32[64,2048]{1,0:T(8,128)} custom-call(bf16[3,4,2048]{2,1,0:T(4,128)(2,1)} %bitcast.1, bf16[4,768,256]{2,1,0:T(8,128)(2,1)} %w_hbm.1, s32[4,256]{1,0:T(4,128)} %lag_hbm.1, s32[4,8]{1,0:T(4,128)} %gap_hbm.1), custom_call_target="tpu_custom_call" | custom-call | tf_op jit(solution)/shard_map/stack/pallas_call | solution.py:260
  49.3 1.9 %copy.6 = f32[64,2048]{1,0:T(8,128)} copy(f32[64,2048]{1,0:T(8,128)} %stack.1) | data formatting | bytes 1048576
